TPU v7x, 128 devices: a whole 4x4x4 slice. The times are simulated.
128 devices in a mesh: row: 16 (over y, x), col: 8 (over z, core).
Axes of the slice: x: 4, y: 4, z: 4, core: 2. Of those that a mesh axis runs over, the one named last changes fastest.
Arguments:
- s_panel: float32 [16384, 512], P('row', 'col'), may hold values from -1.5 to 1.5
- l_inv: float32 [512, 512], P(None, 'col'), may hold values from -1 to 8, as said below
- h_diag: float32 [512, 512], P(None, 'col'), may hold values from -0.25 to 0.25
- h_panel: float32 [16384, 512], P('row', 'col'), may hold values from -1.5 to 1.5
- h_trail: float32 [16384, 16384], P('row', 'col'), may hold values from -6 to 6
Outputs:
- l_panel: float32 [16384, 512], P('row', 'col')
- h_panel_out: float32 [16384, 512], P('row', 'col')
- h_trail_out: float32 [16384, 16384], P('row', 'col')
Inputs may be any that keep to these rules, and one draw needn't show every extreme that they name: l_inv is lower triangular with a positive diagonal.
All inputs are finite; a program needn't handle non-finite values.
Results may differ from a plain program's by a relative error of at most 0.00021.
Values sent between devices are 32-bit elements; how exact they have to be, the bound alone decides.
A program may use at most 128 MiB of HBM per device.

v0:
```python
import jax
import jax.numpy as jnp
from jax import lax
from jax.sharding import PartitionSpec as P


def from_root(value, axis, root):
    mine = lax.axis_index(axis) == root
    return lax.psum(jnp.where(mine, value, jnp.zeros_like(value)), axis)


def product(first, second):
    return jnp.dot(
        first, second, precision=lax.Precision.HIGHEST, preferred_element_type=jnp.float32
    )


def on_device(s_panel, l_inv, h_diag, h_panel, h_trail):
    share_width = s_panel.shape[1]
    col_pos = lax.axis_index("col")
    offset = col_pos * share_width
    inverse, diag_full = (
        lax.all_gather(l_inv, "col", axis=1, tiled=True),
        lax.all_gather(h_diag, "col", axis=1, tiled=True),
    )
    term_lower = product(s_panel, l_inv.T)
    term_coupled = product(h_panel, l_inv.T)
    lower_rows, coupled = lax.psum((term_lower, term_coupled), "col")
    diag_half = product(inverse, diag_full)
    diag_new = product(diag_half, inverse.T)
    corrected = coupled - product(lower_rows, diag_new)
    lower_share = lax.dynamic_slice_in_dim(lower_rows, offset, share_width, 1)
    corrected_share = lax.dynamic_slice_in_dim(corrected, offset, share_width, 1)
    groups = lax.axis_size("row") // lax.axis_size("col")
    lower_parts = []
    coupled_parts = []
    for member in range(groups):
        source = col_pos * groups + member
        got_lower, got_coupled = (
            from_root(lower_rows, "row", source),
            from_root(coupled, "row", source),
        )
        lower_parts.append(got_lower)
        coupled_parts.append(got_coupled)
    col_lower = jnp.concatenate(lower_parts, axis=0)
    col_coupled = jnp.concatenate(coupled_parts, axis=0)
    left_side = jnp.concatenate([lower_rows, corrected], axis=1)
    right_side = jnp.concatenate([col_coupled, col_lower], axis=1)
    h_trail_out = h_trail - product(left_side, right_side.T)
    return (lower_share, corrected_share, h_trail_out)


def solution(mesh):
    in_specs = (P("row", "col"), P(None, "col"), P(None, "col"), P("row", "col"), P("row", "col"))
    out_specs = (P("row", "col"), P("row", "col"), P("row", "col"))
    return jax.shard_map(
        on_device, mesh=mesh, in_specs=in_specs, out_specs=out_specs, check_vma=False
    )
```

profile of v0, /device:TPU:8, one launch (start us, length us, event | category | flops | bytes accessed | tf_op | source)
XLA Modules:
  0.0 327.0 jit_solution(14757342435422621455)
XLA Ops:
  7.2 0.0 all-reduce.7.cloned.1.call-start
  7.2 0.9 copy-done
  8.1 4.1 %fusion.15 = f32[1024,512]{1,0:T(8,128)} fusion(f32[1024,64]{0,1:T(8,128)S(1)} %copy-done, f32[512,64]{0,1:T(8,128)} %param.6), kind=kOutput, calls=%fused_computation.20 | convolution fusion | flops 402653184 | bytes 2490368 | tf_op jit(solution)/shard_map/dot_general | solution.py:13
  12.2 3.2 fusion.16
  15.4 0.0 all-gather.3.cloned.1.call-start
  15.5 0.7 all-gather.3.cloned.1.call-update
  16.2 0.0 all-gather.5.cloned.1.call-start
  16.2 0.7 all-gather.5.cloned.1.call-update
  16.9 0.2 all-reduce.5.cloned.1.call-start
  17.2 73.8 %all-reduce.7.cloned.1.call-done = (f32[1024,512]{1,0:T(8,128)}, f32[1024,512]{1,0:T(8,128)}) async-done(((f32[1024,512]{1,0:T(8,128)}, f32[1024,512]{1,0:T(8,128)}), (f32[1024,512]{1,0:T(8,128)}, f32[1024,512]{1,0:T(8,128)})) %all-reduce.7.cloned.1.call-update) | async-done | bytes 4194320 | tf_op jit(solution)/shard_map/psum | solution.py:28
  91.0 6.1 %broadcast_select_fusion.1 = (f32[1024,512]{1,0:T(8,128)}, f32[1024,512]{1,0:T(8,128)}, f32[1024,512]{1,0:T(8,128)}, f32[1024,512]{1,0:T(8,128)}) fusion(f32[1024,512]{1,0:T(8,128)} %get-tuple-element.10, pred[]{:T(512)S(6)} %eq.8, pred[]{:T(512)S(6)} %eq.9, f32[1024,512]{1,0:T(8,128)} %get-tuple-element.11), kind=kLoop, calls=%fused_computation.14 | loop fusion | flops 2097152 | bytes 12582914 | tf_op jit(solution)/shard_map/jit(_where)/select_n | solution.py:9
  97.1 0.0 all-reduce.5.cloned.1.call-update
  97.1 19.2 %all-gather.3.cloned.1.call-done = f32[512,512]{0,1:T(8,128)} async-done(((f32[512,64]{0,1:T(8,128)}), f32[512,512]{0,1:T(8,128)}) %all-gather.3.cloned.1.call-update) | async-done | bytes 1048592 | tf_op jit(solution)/shard_map/all_gather | solution.py:23
  116.3 25.2 %all-gather.5.cloned.1.call-done = f32[512,512]{0,1:T(8,128)} async-done(((f32[512,64]{0,1:T(8,128)}), f32[512,512]{0,1:T(8,128)}) %all-gather.5.cloned.1.call-update) | async-done | bytes 1048592 | tf_op jit(solution)/shard_map/all_gather | solution.py:24
  141.5 5.2 %fusion.17 = f32[512,512]{1,0:T(8,128)S(1)} fusion(f32[512,512]{0,1:T(8,128)} %all-gather.3.cloned.1.call-done, f32[512,512]{0,1:T(8,128)} %all-gather.5.cloned.1.call-done), kind=kOutput, calls=%fused_computation.22 | convolution fusion | flops 1610612736 | bytes 3145728 | tf_op jit(solution)/shard_map/dot_general | solution.py:13
  146.7 1.9 fusion.18
  148.6 3.5 %convolution_subtract_fusion = f32[1024,512]{1,0:T(8,128)S(1)} fusion(f32[1024,512]{1,0:T(8,128)S(1)} %copy-done.2, f32[1024,512]{1,0:T(8,128)S(1)} %copy-done.1, f32[512,512]{1,0:T(8,128)S(1)} %fusion.18), kind=kOutput, calls=%fused_computation.12 | convolution fusion | flops 3221749760 | bytes 7340032 | tf_op jit(solution)/shard_map/dot_general | solution.py:13
  152.0 1.3 copy-done.4
  153.4 0.2 constant_dynamic-slice_fusion
  153.6 0.9 copy.10
  154.5 0.2 constant_dynamic-slice_fusion.1
  154.7 0.9 copy.9
  155.6 131.2 %all-reduce.5.cloned.1.call-done = (f32[1024,512]{1,0:T(8,128)}, f32[1024,512]{1,0:T(8,128)}, f32[1024,512]{1,0:T(8,128)}, f32[1024,512]{1,0:T(8,128)}) async-done(((f32[1024,512]{1,0:T(8,128)}, f32[1024,512]{1,0:T(8,128)}, f32[1024,512]{1,0:T(8,128)}, f32[1024,512]{1,0:T(8,128)}), (f32[1024,512]{1,0:T(8,128)}, f32[1024,512]{1,0:T(8,128)}, f32[1024,512]{1,0:T(8,128)}, ...) | async-done | bytes 8388624 | tf_op jit(solution)/shard_map/psum | solution.py:9
  286.8 33.7 %fusion.8 = f32[1024,2048]{1,0:T(8,128)} fusion(f32[1024,2048]{1,0:T(8,128)} %param.9, f32[1024,512]{1,0:T(8,128)} %get-tuple-element.6, f32[1024,512]{1,0:T(8,128)} %get-tuple-element.7, f32[1024,512]{1,0:T(8,128)} %get-tuple-element.8, f32[1024,512]{1,0:T(8,128)} %get-tuple-element.9, f32[1024,512]{1,0:T(8,128)} %copy-done.4, f32[1024,512]{1,0:T(8,128)S(1)} %copy-done.1), kind=kOutput, calls=%fused_computation.8 | convolution fusion | flops 25779240960 | bytes 29360128 | tf_op jit(solution)/shard_map/dot_general | solution.py:13
  (13 shorter events, 0.0 us)
Async XLA Ops:
  7.2 1.0 copy-start
  7.2 5.0 %copy-start.5 = (f32[512,64]{0,1:T(8,128)S(1)}, f32[512,64]{0,1:T(8,128)}, u32[]{:S(2)}) copy-start(f32[512,64]{0,1:T(8,128)} %param.6) | copy-start | bytes 393220
  7.2 5.0 %copy-start.6 = (f32[1024,64]{0,1:T(8,128)S(1)}, f32[1024,64]{0,1:T(8,128)}, u32[]{:S(2)}) copy-start(f32[1024,64]{0,1:T(8,128)} %param.8) | copy-start | bytes 786436
  7.2 83.8 %all-reduce.7.cloned.1.call-start = ((), (), s32[]{:S(2)}) async-start(), calls=%async_computation.3 | async-start | bytes 8388608 | tf_op jit(solution)/shard_map/psum | solution.py:28
  15.4 100.8 %all-gather.3.cloned.1.call-start = ((), (), s32[]{:S(2)}) async-start(), calls=%async_computation | async-start | bytes 1179648 | tf_op jit(solution)/shard_map/all_gather | solution.py:23
  16.2 125.3 %all-gather.5.cloned.1.call-start = ((), (), s32[]{:S(2)}) async-start(), calls=%async_computation.1 | async-start | bytes 1179648 | tf_op jit(solution)/shard_map/all_gather | solution.py:24
  16.9 269.9 %all-reduce.5.cloned.1.call-start = ((), (), s32[]{:S(2)}) async-start(), calls=%async_computation.2 | async-start | bytes 16777216 | tf_op jit(solution)/shard_map/psum | solution.py:9
  116.3 30.4 %copy-start.3 = (f32[512,512]{0,1:T(8,128)S(1)}, f32[512,512]{0,1:T(8,128)}, u32[]{:S(2)}) copy-start(f32[512,512]{0,1:T(8,128)} %all-gather.3.cloned.1.call-done) | copy-start | bytes 3145732
  141.5 7.1 %copy-start.2 = (f32[1024,512]{1,0:T(8,128)S(1)}, f32[1024,512]{1,0:T(8,128)}, u32[]{:S(2)}) copy-start(f32[1024,512]{1,0:T(8,128)} %get-tuple-element.11) | copy-start | bytes 6291460
  146.7 1.9 copy-start.1
  152.0 1.3 copy-start.4
Sparse Core Ops, SparseCore 0:
  15.5 75.3 all-reduce.6
  92.7 23.5 all-gather.2
  118.0 23.4 all-gather.4
  145.9 140.8 all-reduce.4
where the time goes:
time: 329 us; the launch traced here: 327 us
  waiting for transfers between devices  251 us (76%)
  matrix products  51.4 us (16%)
  between operations  13.9 us (4%)
  other arithmetic  6.1 us (2%)
  local copies, waits for them, and re-layouts  4.41 us (1%)
    psum x1, waiting for transfers between devices, from_root(): return lax.psum(jnp.where(mine, value, jnp.zeros_like(value)), axis)  131 us
    psum x1, waiting for transfers between devices, on_device(): lower_rows, coupled = lax.psum((term_lower, term_coupled), 'col')  73.8 us
    dot_general x6, matrix products, product(): jnp.dot(first, second, precision=lax.Precision.HIGHEST, preferred_element...  51.4 us
    all_gather x1, waiting for transfers between devices, on_device(): lax.all_gather(h_diag, 'col', axis=1, tiled=True)  25.2 us
    all_gather x1, waiting for transfers between devices, on_device(): lax.all_gather(l_inv, 'col', axis=1, tiled=True)  19.2 us
  transfers between devices with their start and end apart: 4, of which 4 were waited for; matrix products, arithmetic and copies ran while one was open for 6% of the time, Pallas kernels for 0%

commit v1 on v0

v1 whole, which is shorter than its diff:
```python
import functools

import jax
import jax.numpy as jnp
from jax import lax
from jax.experimental import pallas as pl
from jax.experimental.pallas import tpu as pltpu
from jax.sharding import PartitionSpec as P

MESH = pl.DeviceIdType.MESH
F32, BF16 = jnp.float32, jnp.bfloat16
ROWS, NB, SIDE = 1024, 512, 64
UNIT = 64
NW = ROWS // UNIT
UNITS = 64
HOP = 5
LEAD = 4
GAP = 3
LAST = UNITS + LEAD + GAP + 4 * HOP
W_STEP = 12
W_FAR, W_DONE = W_STEP + 5, W_STEP + 8
Q_STEP = W_DONE
U_STEP = 55
U_READY = LAST - 42


def split(value):
    high = value.astype(BF16)
    return high, (value - high.astype(F32)).astype(BF16)


def dot3(a_high, a_low, b_high, b_low, b_dim):
    dims = (((1,), (b_dim,)), ((), ()))
    one = lambda a, b: lax.dot_general(a, b, dims, preferred_element_type=F32)
    return one(a_high, b_high) + (one(a_high, b_low) + one(a_low, b_high))


def half_turn(tile):
    return pltpu.roll(tile, SIDE, 1)


def kernel(s_ref, x_ref, d_ref, p_ref, t_hbm, low_ref, red_ref, out_hbm,
           w_all, xh_all, items, trail, left_high, left_low, q_high, q_low,
           x_high, x_low, xt_high, xt_low, m_high, m_low, n_high, n_low,
           d_full, z_high, z_low, a_high, a_low, b_high, b_low,
           own_recv, z_recv, far_recv, sib_recv, item_recv,
           xz_recv, xf_recv, xs_recv, own_send, sib_send, x_send, item_send,
           load_sem, store_sem):
    r, j = lax.axis_index("row"), lax.axis_index("col")
    y, x, z, c = r // 4, r % 4, j // 2, j % 2
    z_up, z_down, z_far = ((z + 1) % 4) * 2 + c, ((z + 3) % 4) * 2 + c, ((z + 2) % 4) * 2 + c
    j_sib = z * 2 + 1 - c
    up, down, sib = (r, z_up), (r, z_down), (r, j_sib)
    plane = [
        (y * 4 + (x + 1) % 4, j), (y * 4 + (x + 3) % 4, j),
        (((y + 1) % 4) * 4 + x, j), (((y + 3) % 4) * 4 + x, j),
    ]
    barrier = pltpu.get_barrier_semaphore()
    for device in plane + [up, down, sib]:
        pl.semaphore_signal(barrier, inc=1, device_id=device, device_id_type=MESH)

    load = pltpu.make_async_copy(t_hbm, trail, load_sem)
    load.start()
    lanes = lambda k: pl.ds(pl.multiple_of(k * 128, 128), 128)
    lane = lambda rows, width=128: lax.broadcasted_iota(jnp.int32, (rows, width), 1)
    xh_all[:, lanes(j)] = jnp.concatenate([x_ref[...], d_ref[...]], axis=1)
    w_all[:, lanes(j)] = jnp.concatenate([s_ref[...], p_ref[...]], axis=1)
    pl.semaphore_wait(barrier, 7)

    def send(ref, send_sem, recv_sem, device):
        return pltpu.make_async_remote_copy(
            src_ref=ref, dst_ref=ref, send_sem=send_sem, recv_sem=recv_sem,
            device_id=device, device_id_type=MESH)

    def arrived(ref, sem):
        send(ref, sib_send.at[0], sem, sib).wait_recv()

    def rows_of(w):
        return pl.ds(pl.multiple_of(w * UNIT, UNIT), UNIT)

    def chunk(w, k):
        return w_all.at[rows_of(w), lanes(k)]

    f = (y + 4 - z) % 4
    outs, depth = [], []
    for m in range(2):
        e = (x + 4 - (2 * c + m)) % 4
        at = lambda a, b, e=e: (e == a) & (f == b)
        to_x = at(0, 0) | at(1, 1) | at(3, 3) | at(1, 2)
        to_up = at(1, 0) | at(1, 1) | at(1, 2)
        to_down = at(3, 0) | at(3, 3) | at(3, 2) | at(2, 1)
        outs.append([to_x, to_x, to_up, to_down])
        third = at(0, 3) | at(2, 3) | at(0, 1) | at(3, 2) | at(2, 1) | at(1, 2)
        depth.append(jnp.where(at(0, 0), 0, jnp.where(
            at(1, 0) | at(3, 0), 1, jnp.where(at(1, 1) | at(3, 3), 2, jnp.where(third, 3, 4)))))

    def unit(q):
        late = q >= 16
        block = jnp.where(late, (q + 32) // 3 - 16, q)
        which = (q + 32) % 3
        slot = jnp.where(late, jnp.where(which == 0, z + 3, jnp.where(which == 1, z + 1, z + 2)), z) % 4
        return rows_of(block), pl.ds(pl.multiple_of(slot * 256, 256), 256)

    def unit_at(t):
        early = t < LEAD + 16
        late = t >= LEAD + 16 + GAP
        return jnp.where(late, t - LEAD - GAP, t - LEAD), (t >= LEAD) & (early | (late & (t < LEAD + GAP + UNITS)))

    own_x = xh_all.at[:, lanes(j)]
    send(own_x, sib_send.at[2], xs_recv, sib).start()
    send(own_x, x_send.at[0], xz_recv.at[0], up).start()
    send(own_x, x_send.at[1], xz_recv.at[1], down).start()

    def prepare():
        for p in range(4):
            at_p, first, second = pl.ds(p * 128, 128), xh_all[:, 256 * p:256 * p + 128], xh_all[:, 256 * p + 128:256 * p + 256]
            lower = lane(NB) < SIDE
            xv = jnp.where(lower, first, half_turn(second))
            dv = jnp.where(lower, half_turn(first), second)
            x_high[:, at_p], x_low[:, at_p] = split(xv)
            m_high[:, at_p], m_low[:, at_p] = split(dv)
            xt_high[at_p, :], xt_low[at_p, :] = split(jnp.transpose(xv))
            z_first = jnp.where(lower, 0.0, half_turn(xv))
            z_second = jnp.where(lower, 0.0, xv)
            z_high[:, 256 * p:256 * p + 128], z_low[:, 256 * p:256 * p + 128] = split(z_first)
            z_high[:, 256 * p + 128:256 * p + 256], z_low[:, 256 * p + 128:256 * p + 256] = split(z_second)

    def half_product():
        value = dot3(x_high[...], x_low[...], m_high[...], m_low[...], 0)
        n_high[...], n_low[...] = split(value)

    def diag_product():
        value = dot3(n_high[...], n_low[...], xt_high[...], xt_low[...], 0)
        d_full[...] = value
        m_high[...], m_low[...] = split(value)

    def inner_product():
        value = dot3(m_high[...], m_low[...], x_high[...], x_low[...], 0)
        lower = lane(NB) < SIDE
        for p in range(4):
            tile = value[:, 128 * p:128 * p + 128]
            for h in range(2):
                at_h = pl.ds(256 * p + 128 * h, 128)
                part = jnp.where(lower, -(tile if h == 0 else half_turn(tile)), 0.0)
                high, low = split(part)
                z_high[:, at_h] = jnp.where(lower, high, z_high[:, at_h])
                z_low[:, at_h] = jnp.where(lower, low, z_low[:, at_h])
        mine = d_full[:, pl.ds(pl.multiple_of(z * 128, 128), 128)]
        mine = jnp.where(c == 0, half_turn(mine), mine)
        row_id = lax.broadcasted_iota(jnp.int32, (NB, 128), 0)
        pick = jnp.where(row_id == lane(NB) + SIDE * j, 1.0, 0.0)
        z_high[:, 1024:1152], z_low[:, 1024:1152] = split(jnp.where(lower, pick, -mine))

    def weights(n, wide):
        at_n = pl.ds(1024, 128) if not wide else pl.ds(pl.multiple_of(n * 256, 256), 256)
        value = dot3(xt_high[...], xt_low[...], z_high[:, at_n], z_low[:, at_n], 0)
        lower = lane(NB) < SIDE
        if wide:
            turned = jnp.concatenate(
                [jnp.where(lower, half_turn(value[:, h * 128:h * 128 + 128]), 0.0) for h in range(2)], axis=1)
        else:
            turned = jnp.where(lower, 0.0, half_turn(value))
        for part, shift in ((value, 0), (turned, SIDE)):
            high, low = split(part)
            for k in range(8):
                q_high[k * 128 + shift:k * 128 + shift + SIDE, at_n] = high[k * SIDE:(k + 1) * SIDE]
                q_low[k * 128 + shift:k * 128 + shift + SIDE, at_n] = low[k * SIDE:(k + 1) * SIDE]

    def left_task(g, n):
        rows = pl.ds(pl.multiple_of(g * 256, 256), 256)

        @pl.when(n == 0)
        def _():
            a_high[...], a_low[...] = split(w_all[rows, :])

        @pl.when(n < 4)
        def _():
            at_n = pl.ds(pl.multiple_of(n * 256, 256), 256)
            value = dot3(a_high[...], a_low[...], q_high[:, at_n], q_low[:, at_n], 0)
            left_high[rows, at_n], left_low[rows, at_n] = split(value)

        @pl.when(n == 4)
        def _():
            value = dot3(a_high[...], a_low[...], q_high[:, 1024:1152], q_low[:, 1024:1152], 0)
            low_ref[rows, :] = value[:, :SIDE]
            red_ref[rows, :] = half_turn(value)[:, :SIDE]

    def store(block, m):
        cols = pl.ds(pl.multiple_of(m * ROWS + block * 128, 128), 128)
        return pltpu.make_async_copy(trail.at[:, cols], out_hbm.at[:, cols], store_sem)

    def trail_task(block, i):
        @pl.when(i == 0)
        def _():
            for m in range(2):
                value = items[m, pl.ds(pl.multiple_of(block * 128, 128), 128), :]
                b_high[m * 128:m * 128 + 128, :], b_low[m * 128:m * 128 + 128, :] = split(value)

        rows = pl.ds(pl.multiple_of(i * 256, 256), 256)
        value = dot3(left_high[rows, :], left_low[rows, :], b_high[...], b_low[...], 1)
        for m in range(2):
            cols = pl.ds(pl.multiple_of(m * ROWS + block * 128, 128), 128)
            trail[rows, cols] = trail[rows, cols] - value[:, m * 128:m * 128 + 128]

        @pl.when(i == 3)
        def _():
            for m in range(2):
                store(block, m).start()

    def step(t, carry):
        @pl.when(t < 8)
        def _():
            for i in range(2):
                w = t * 2 + i
                send(chunk(w, j), sib_send.at[0], own_recv.at[w], sib).start()
                send(chunk(w, j), own_send.at[0], z_recv.at[0, w], up).start()
                send(chunk(w, j), own_send.at[1], z_recv.at[1, w], down).start()

        @pl.when((t >= 2) & (t < 2 + NW))
        def _():
            arrived(chunk(t - 2, j_sib), own_recv.at[t - 2])

        for m in range(2):
            q_copy, ready = unit_at(t + 2)

            @pl.when((depth[m] == 0) & ready)
            def _():
                at = unit(q_copy)
                pltpu.make_async_copy(w_all.at[at[0], at[1]], items.at[m, at[0], at[1]], item_recv.at[m, q_copy]).start()

            q, here = unit_at(t - HOP * depth[m])

            @pl.when(here)
            def _():
                at = unit(q)
                part = items.at[m, at[0], at[1]]
                arrived(part, item_recv.at[m, q])
                for d in range(4):
                    @pl.when(outs[m][d])
                    def _():
                        send(part, item_send.at[m, d], item_recv.at[m, q], plane[d]).start()

        @pl.when((t >= W_STEP) & (t < W_STEP + 2 * NW) & ((t - W_STEP) % 2 == 0))
        def _():
            w = (t - W_STEP) // 2
            arrived(chunk(w, z_down), z_recv.at[0, w])
            arrived(chunk(w, z_up), z_recv.at[1, w])

            @pl.when(c == 0)
            def _():
                send(chunk(w, z_down), own_send.at[2], far_recv.at[w], up).start()

            @pl.when(c == 1)
            def _():
                send(chunk(w, z_up), own_send.at[2], far_recv.at[w], down).start()

            send(chunk(w, z_down), sib_send.at[1], sib_recv.at[w], sib).start()
            send(chunk(w, z_up), sib_send.at[1], sib_recv.at[w], sib).start()

        @pl.when((t >= W_FAR) & (t < W_FAR + 2 * NW) & ((t - W_FAR) % 2 == 0))
        def _():
            w = (t - W_FAR) // 2
            arrived(chunk(w, z_far), far_recv.at[w])
            send(chunk(w, z_far), sib_send.at[1], sib_recv.at[w], sib).start()

        @pl.when((t >= W_DONE) & (t < W_DONE + 2 * NW) & ((t - W_DONE) % 2 == 0))
        def _():
            w = (t - W_DONE) // 2
            arrived(w_all.at[rows_of(w), pl.ds(0, 384)], sib_recv.at[w])

        @pl.when(t == W_STEP - 1)
        def _():
            first, second = xh_all.at[:, lanes(z_down)], xh_all.at[:, lanes(z_up)]
            arrived(first, xz_recv.at[0])
            arrived(second, xz_recv.at[1])

            @pl.when(c == 0)
            def _():
                send(first, x_send.at[2], xf_recv, up).start()

            @pl.when(c == 1)
            def _():
                send(second, x_send.at[2], xf_recv, down).start()

            send(first, sib_send.at[2], xs_recv, sib).start()
            send(second, sib_send.at[2], xs_recv, sib).start()

        @pl.when(t == W_FAR - 1)
        def _():
            far = xh_all.at[:, lanes(z_far)]
            arrived(far, xf_recv)
            send(far, sib_send.at[2], xs_recv, sib).start()

        @pl.when(t == Q_STEP)
        def _():
            arrived(xh_all.at[:, pl.ds(0, 512)], xs_recv)
            prepare()

        pl.when(t == Q_STEP + 1)(half_product)
        pl.when(t == Q_STEP + 2)(diag_product)
        pl.when(t == Q_STEP + 3)(inner_product)

        @pl.when((t >= Q_STEP + 4) & (t < Q_STEP + 8))
        def _():
            weights(t - Q_STEP - 4, True)

        pl.when(t == Q_STEP + 8)(lambda: weights(0, False))

        for g in range(4):
            start = max(Q_STEP + 9, W_DONE + 6 + 8 * g)

            @pl.when((t >= start) & (t < start + 5))
            def _():
                left_task(g, t - start)

        @pl.when(t == U_STEP - 1)
        def _():
            pltpu.make_async_copy(t_hbm, trail, load_sem).wait()

        dense = t < U_STEP + 16
        block = jnp.where(dense, (t - U_STEP) // 4, (t - U_READY) // 6)
        i = jnp.where(dense, (t - U_STEP) % 4, (t - U_READY) % 6)

        @pl.when((t >= U_STEP) & (dense | (block >= 4)) & (i < 4))
        def _():
            trail_task(block, i)

        return carry

    lax.fori_loop(0, LAST, step, 0)
    lax.fori_loop(0, 4, lambda i, carry: (trail_task(7, i), carry)[1], 0)

    own = w_all.at[:, lanes(j)]
    done = lambda ref, sem: send(ref, sem, own_recv.at[0], sib).wait_send()
    for i in range(3):
        done(own, own_send.at[i])
        done(own_x, x_send.at[i])
    done(own, sib_send.at[0])
    done(w_all.at[:, pl.ds(0, 384)], sib_send.at[1])
    done(xh_all.at[:, pl.ds(0, 512)], sib_send.at[2])
    for m in range(2):
        for d in range(4):
            @pl.when(outs[m][d])
            def _():
                done(items.at[m], item_send.at[m, d])
    pltpu.make_async_copy(trail, out_hbm, store_sem).wait()


def on_device(s_panel, l_inv, h_diag, h_panel, h_trail):
    vmem = pl.BlockSpec(memory_space=pltpu.VMEM)
    hbm = pl.BlockSpec(memory_space=pl.ANY)
    dma = pltpu.SemaphoreType.DMA
    mats = [pltpu.VMEM((NB, NB), BF16)] * 8
    return pl.pallas_call(
        kernel,
        out_shape=(
            jax.ShapeDtypeStruct(s_panel.shape, F32),
            jax.ShapeDtypeStruct(h_panel.shape, F32),
            jax.ShapeDtypeStruct(h_trail.shape, F32),
        ),
        in_specs=[vmem, vmem, vmem, vmem, hbm],
        out_specs=(vmem, vmem, hbm),
        scratch_shapes=[
            pltpu.VMEM((ROWS, 1024), F32), pltpu.VMEM((NB, 1024), F32),
            pltpu.VMEM((2, ROWS, 1024), F32), pltpu.VMEM((ROWS, 2 * ROWS), F32),
            pltpu.VMEM((ROWS, 1024), BF16), pltpu.VMEM((ROWS, 1024), BF16),
            pltpu.VMEM((1024, 1152), BF16), pltpu.VMEM((1024, 1152), BF16),
            *mats,
            pltpu.VMEM((NB, NB), F32), pltpu.VMEM((NB, 1152), BF16), pltpu.VMEM((NB, 1152), BF16),
            *[pltpu.VMEM((256, 1024), BF16)] * 4,
            dma((NW,)), dma((2, NW)), dma((NW,)), dma((NW,)), dma((2, UNITS)),
            dma((2,)), dma, dma, dma((3,)), dma((3,)), dma((3,)), dma((2, 4)),
            dma, dma,
        ],
        compiler_params=pltpu.CompilerParams(
            collective_id=0, has_side_effects=True, vmem_limit_bytes=56 * 2**20),
        cost_estimate=pl.CostEstimate(flops=22 * 10**9, bytes_accessed=20 * 2**20, transcendentals=0),
    )(s_panel, l_inv, h_diag, h_panel, h_trail)


def solution(mesh):
    in_specs = (P("row", "col"), P(None, "col"), P(None, "col"), P("row", "col"), P("row", "col"))
    out_specs = (P("row", "col"), P("row", "col"), P("row", "col"))
    return jax.shard_map(
        on_device, mesh=mesh, in_specs=in_specs, out_specs=out_specs, check_vma=False
    )
```

time: 329 us -> 123 us (0.37)
  waiting for transfers between devices: 251 us -> 0 us
  Pallas kernels: 0 us -> 101 us
  matrix products: 51.4 us -> 0 us
  local copies, waits for them, and re-layouts: 4.41 us -> 19.2 us
  between operations: 13.9 us -> 0.64 us
  other arithmetic: 6.1 us -> 0 us
    psum x2 -> x0, waiting for transfers between devices: 205 us -> none  [the longest x1 131 us: from_root(): return lax.psum(jnp.where(mine, value, jnp.zeros_like(value)), axis)]
    pallas_call x0 -> x1, Pallas kernels: none -> 101 us  [on_device(): pl.pallas_call(kernel, out_shape=(jax.ShapeDtypeStruct(s_panel.shape, F32...]
    dot_general x6 -> x0, matrix products: 51.4 us -> none  [product(): jnp.dot(first, second, precision=lax.Precision.HIGHEST, preferred_element...]
    all_gather x2 -> x0, waiting for transfers between devices: 44.4 us -> none  [the longest x1 25.2 us: on_device(): lax.all_gather(h_diag, 'col', axis=1, tiled=True)]
    unnamed x16 -> x5, local copies, waits for them, and re-layouts: 4.01 us -> 15.3 us
    select_n x1 -> x0, other arithmetic: 6.1 us -> none  [from_root(): return lax.psum(jnp.where(mine, value, jnp.zeros_like(value)), axis)]
    pallas_call x0 -> x2, local copies, waits for them, and re-layouts: none -> 3.86 us  [on_device(): pl.pallas_call(kernel, out_shape=(jax.ShapeDtypeStruct(s_panel.shape, F32...]
  transfers between devices with their start and end apart: 4 -> 0, of which waited for: 4 -> 0; matrix products, arithmetic and copies ran while one was open for 6% -> 0% of each run, Pallas kernels for 0% -> 0%
where the time goes in v1:
time: 123 us; the launch traced here: 121 us
  Pallas kernels  101 us (82%)
  local copies, waits for them, and re-layouts  19.2 us (16%)
    pallas_call x1, Pallas kernels, on_device(): pl.pallas_call(kernel, out_shape=(jax.ShapeDtypeStruct(s_panel.shape, F32...  101 us
    unnamed x5, local copies, waits for them, and re-layouts  15.3 us
    pallas_call x2, local copies, waits for them, and re-layouts, on_device(): pl.pallas_call(kernel, out_shape=(jax.ShapeDtypeStruct(s_panel.shape, F32...  3.86 us

profile of v1, /device:TPU:8, one launch (start us, length us, event | category | flops | bytes accessed | tf_op | source)
XLA Modules:
  0.0 120.9 jit_solution(14061912466380300521)
XLA Ops:
  0.6 1.7 %copy.9.x_ref = f32[512,64]{1,0:T(8,128)} copy(f32[512,64]{0,1:T(8,128)} %param.6) | data formatting | bytes 262144 | tf_op args[1]
  2.4 1.7 %copy.10.d_ref = f32[512,64]{1,0:T(8,128)} copy(f32[512,64]{0,1:T(8,128)} %param.7) | data formatting | bytes 262144 | tf_op args[2]
  4.1 1.9 %copy.8.s_ref = f32[1024,64]{1,0:T(8,128)} copy(f32[1024,64]{0,1:T(8,128)} %param.5) | data formatting | bytes 524288 | tf_op args[0]
  6.1 2.0 %copy.11.p_ref = f32[1024,64]{1,0:T(8,128)} copy(f32[1024,64]{0,1:T(8,128)} %param.8) | data formatting | bytes 524288 | tf_op args[3]
  8.1 101.1 %shard_map.76 = (f32[1024,64]{1,0:T(8,128)}, f32[1024,64]{1,0:T(8,128)}, f32[1024,2048]{1,0:T(8,128)}) custom-call(f32[1024,64]{1,0:T(8,128)} %copy.8.s_ref, f32[512,64]{1,0:T(8,128)} %copy.9.x_ref, f32[512,64]{1,0:T(8,128)} %copy.10.d_ref, f32[1024,64]{1,0:T(8,128)} %copy.11.p_ref, f32[1024,2048]{1,0:T(8,128)} %t_hbm.1), custom_call_target="tpu_custom_call" | custom-call | flops 22000001024 | bytes 20971520 | tf_op jit(solution)/shard_map/pallas_call | solution.py:354
  109.1 1.9 %copy.12 = f32[1024,64]{0,1:T(8,128)} copy(f32[1024,64]{1,0:T(8,128)} %get-tuple-element.3) | data formatting | bytes 524288 | tf_op jit(solution)/shard_map/pallas_call | solution.py:354
  111.1 1.9 %copy.13 = f32[1024,64]{0,1:T(8,128)} copy(f32[1024,64]{1,0:T(8,128)} %get-tuple-element.4) | data formatting | bytes 524288 | tf_op jit(solution)/shard_map/pallas_call | solution.py:354
  113.0 7.9 %copy.15 = f32[1024,2048]{1,0:T(8,128)} copy(f32[1024,2048]{1,0:T(8,128)} %get-tuple-element.11) | data formatting | bytes 16777216

commit v2 on v1

v2 whole, which is shorter than its diff:
```python
import functools

import jax
import jax.numpy as jnp
from jax import lax
from jax.experimental import pallas as pl
from jax.experimental.pallas import tpu as pltpu
from jax.sharding import PartitionSpec as P

MESH = pl.DeviceIdType.MESH
F32, BF16 = jnp.float32, jnp.bfloat16
ROWS, NB, SIDE = 1024, 512, 64
NW = ROWS // 128
UNITS = 64
HOP = 5
LEAD = 4
GAP = 3
LAST = UNITS + LEAD + GAP + 4 * HOP
W_STEP = 12
W_FAR, W_DONE = W_STEP + 5, W_STEP + 8
W_OPEN = 2
X_STEP, X_FAR = W_STEP - 1, W_STEP + 4
Q_STEP = W_DONE
U_READY = LAST - 42


def split(value):
    high = value.astype(BF16)
    return high, (value - high.astype(F32)).astype(BF16)


def dot3(a_high, a_low, b_high, b_low, b_dim):
    dims = (((1,), (b_dim,)), ((), ()))
    one = lambda a, b: lax.dot_general(a, b, dims, preferred_element_type=F32)
    return one(a_high, b_high) + (one(a_high, b_low) + one(a_low, b_high))


def half_turn(tile):
    return pltpu.roll(tile, SIDE, 1)


def kernel(s_hbm, x_hbm, d_hbm, p_hbm, t_hbm, low_ref, red_ref, trail,
           w_all, xh_all, items, left_high, left_low, q_high, q_low,
           x_high, x_low, xt_high, xt_low, m_high, m_low, n_high, n_low,
           d_full, z_high, z_low, a_high, a_low, b_high, b_low,
           own_recv, z_recv, far_recv, sib_recv, item_recv,
           xz_recv, xf_recv, xs_recv, own_send, sib_send, x_send, item_send,
           fetch_sem, load_sem):
    r, j = lax.axis_index("row"), lax.axis_index("col")
    y, x, z, c = r // 4, r % 4, j // 2, j % 2
    z_up, z_down, z_far = ((z + 1) % 4) * 2 + c, ((z + 3) % 4) * 2 + c, ((z + 2) % 4) * 2 + c
    j_sib = z * 2 + 1 - c
    up, down, sib = (r, z_up), (r, z_down), (r, j_sib)
    plane = [
        (y * 4 + (x + 1) % 4, j), (y * 4 + (x + 3) % 4, j),
        (((y + 1) % 4) * 4 + x, j), (((y + 3) % 4) * 4 + x, j),
    ]
    barrier = pltpu.get_barrier_semaphore()
    for device in plane + [up, down, sib]:
        pl.semaphore_signal(barrier, inc=1, device_id=device, device_id_type=MESH)

    slot = lambda k: pl.ds(pl.multiple_of(k * 128, 128), 128)
    lane = lambda rows, width=128: lax.broadcasted_iota(jnp.int32, (rows, width), 1)
    fetches = []
    for h, (panel, matrix) in enumerate(((s_hbm, x_hbm), (p_hbm, d_hbm))):
        at_h = pl.ds(pl.multiple_of(j * 128 + h * SIDE, SIDE), SIDE)
        fetches.append(pltpu.make_async_copy(matrix, xh_all.at[at_h, :], fetch_sem.at[8, h]))
        for w in range(NW):
            fetches.append(pltpu.make_async_copy(
                panel.at[:, pl.ds(w * 128, 128)], w_all.at[w, at_h, :], fetch_sem.at[w, h]))
    for fetch in fetches:
        fetch.start()
    load = pltpu.make_async_copy(t_hbm, trail, load_sem)
    load.start()
    for fetch in fetches:
        fetch.wait()
    pl.semaphore_wait(barrier, 7)

    def send(ref, send_sem, recv_sem, device):
        return pltpu.make_async_remote_copy(
            src_ref=ref, dst_ref=ref, send_sem=send_sem, recv_sem=recv_sem,
            device_id=device, device_id_type=MESH)

    def arrived(ref, sem):
        send(ref, sib_send.at[0], sem, sib).wait_recv()

    def chunk(w, k):
        return w_all.at[w, slot(k), :]

    f = (y + 4 - z) % 4
    outs, depth = [], []
    for m in range(2):
        e = (x + 4 - (2 * c + m)) % 4
        at = lambda a, b, e=e: (e == a) & (f == b)
        to_x = at(0, 0) | at(1, 1) | at(3, 3) | at(1, 2)
        to_up = at(1, 0) | at(1, 1) | at(1, 2)
        to_down = at(3, 0) | at(3, 3) | at(3, 2) | at(2, 1)
        outs.append([to_x, to_x, to_up, to_down])
        third = at(0, 3) | at(2, 3) | at(0, 1) | at(3, 2) | at(2, 1) | at(1, 2)
        depth.append(jnp.where(at(0, 0), 0, jnp.where(
            at(1, 0) | at(3, 0), 1, jnp.where(at(1, 1) | at(3, 3), 2, jnp.where(third, 3, 4)))))

    def unit(q):
        late = q >= 16
        block = jnp.where(late, (q + 32) // 6 - 8, q // 2)
        which = (q + 32) % 6 // 2
        level = jnp.where(late, jnp.where(which == 0, z + 3, jnp.where(which == 1, z + 1, z + 2)), z) % 4
        return block, slot(level * 2 + q % 2)

    def unit_at(t):
        early = t < LEAD + 16
        late = t >= LEAD + 16 + GAP
        return jnp.where(late, t - LEAD - GAP, t - LEAD), (t >= LEAD) & (early | (late & (t < LEAD + GAP + UNITS)))

    own_x = xh_all.at[slot(j), :]
    send(own_x, sib_send.at[2], xs_recv, sib).start()
    send(own_x, x_send.at[0], xz_recv.at[0], up).start()
    send(own_x, x_send.at[1], xz_recv.at[1], down).start()

    def prepare():
        lower = lane(NB) < SIDE
        for p in range(4):
            rows = pl.ds(p * 128, 128)
            pair = [xh_all[256 * p + 128 * h:256 * p + 128 * h + 128, :] for h in range(2)]
            xt = jnp.concatenate([tile[:SIDE] for tile in pair], axis=0)
            dt = jnp.concatenate([tile[SIDE:] for tile in pair], axis=0)
            xt_high[rows, :], xt_low[rows, :] = split(xt)
            m_high[rows, :], m_low[rows, :] = split(dt)
            xv = jnp.transpose(xt)
            x_high[:, rows], x_low[:, rows] = split(xv)
            first, second = pl.ds(256 * p, 128), pl.ds(256 * p + 128, 128)
            z_high[:, first], z_low[:, first] = split(jnp.where(lower, 0.0, half_turn(xv)))
            z_high[:, second], z_low[:, second] = split(jnp.where(lower, 0.0, xv))

    def half_product():
        value = dot3(x_high[...], x_low[...], m_high[...], m_low[...], 1)
        n_high[...], n_low[...] = split(value)

    def diag_product():
        value = dot3(n_high[...], n_low[...], xt_high[...], xt_low[...], 0)
        d_full[...] = value
        m_high[...], m_low[...] = split(value)

    def inner_product():
        value = dot3(m_high[...], m_low[...], x_high[...], x_low[...], 0)
        lower = lane(NB) < SIDE
        for p in range(4):
            tile = value[:, 128 * p:128 * p + 128]
            for h in range(2):
                at_h = pl.ds(256 * p + 128 * h, 128)
                part = jnp.where(lower, -(tile if h == 0 else half_turn(tile)), 0.0)
                high, low = split(part)
                z_high[:, at_h] = jnp.where(lower, high, z_high[:, at_h])
                z_low[:, at_h] = jnp.where(lower, low, z_low[:, at_h])
        mine = d_full[:, pl.ds(pl.multiple_of(z * 128, 128), 128)]
        mine = jnp.where(c == 0, half_turn(mine), mine)
        row_id = lax.broadcasted_iota(jnp.int32, (NB, 128), 0)
        pick = jnp.where(row_id == lane(NB) + SIDE * j, 1.0, 0.0)
        z_high[:, 1024:1152], z_low[:, 1024:1152] = split(jnp.where(lower, pick, -mine))

    def weights(n, wide):
        at_n = pl.ds(1024, 128) if not wide else pl.ds(pl.multiple_of(n * 256, 256), 256)
        value = dot3(xt_high[...], xt_low[...], z_high[:, at_n], z_low[:, at_n], 0)
        lower = lane(NB) < SIDE
        if wide:
            turned = jnp.concatenate(
                [jnp.where(lower, half_turn(value[:, h * 128:h * 128 + 128]), 0.0) for h in range(2)], axis=1)
        else:
            turned = jnp.where(lower, 0.0, half_turn(value))
        for part, shift in ((value, 0), (turned, SIDE)):
            high, low = split(part)
            for k in range(8):
                q_high[k * 128 + shift:k * 128 + shift + SIDE, at_n] = high[k * SIDE:(k + 1) * SIDE]
                q_low[k * 128 + shift:k * 128 + shift + SIDE, at_n] = low[k * SIDE:(k + 1) * SIDE]

    def left_task(g, n):
        rows = pl.ds(pl.multiple_of(g * 256, 256), 256)

        @pl.when(n == 0)
        def _():
            for h in range(2):
                a_high[h * 128:h * 128 + 128, :], a_low[h * 128:h * 128 + 128, :] = split(
                    jnp.transpose(w_all[2 * g + h]))

        @pl.when(n < 4)
        def _():
            at_n = pl.ds(pl.multiple_of(n * 256, 256), 256)
            value = dot3(a_high[...], a_low[...], q_high[:, at_n], q_low[:, at_n], 0)
            left_high[rows, at_n], left_low[rows, at_n] = split(value)

        @pl.when(n == 4)
        def _():
            value = dot3(a_high[...], a_low[...], q_high[:, 1024:1152], q_low[:, 1024:1152], 0)
            turned = jnp.transpose(value)
            low_ref[:, rows] = turned[:SIDE]
            red_ref[:, rows] = turned[SIDE:]

    def trail_task(block, i):
        if i == 0:
            for m in range(2):
                cols = pl.ds(m * 128, 128)
                b_high[:, cols], b_low[:, cols] = split(items[m, block])

        rows = pl.ds(i * 256, 256)
        value = dot3(left_high[rows, :], left_low[rows, :], b_high[...], b_low[...], 0)
        for m in range(2):
            cols = pl.ds(pl.multiple_of(m * ROWS + block * 128, 128), 128)
            trail[rows, cols] = trail[rows, cols] - value[:, m * 128:m * 128 + 128]

    def send_along(w):
        send(chunk(w, j), own_send.at[0], z_recv.at[0, w], up).start()
        send(chunk(w, j), own_send.at[1], z_recv.at[1, w], down).start()

    def tree(t):
        for m in range(2):
            q_copy, ready = unit_at(t + 2)

            @pl.when((depth[m] == 0) & ready)
            def _():
                at = unit(q_copy)
                pltpu.make_async_copy(
                    w_all.at[at[0], at[1], :], items.at[m, at[0], at[1], :], item_recv.at[m, q_copy]).start()

            q, here = unit_at(t - HOP * depth[m])

            @pl.when(here)
            def _():
                at = unit(q)
                part = items.at[m, at[0], at[1], :]
                arrived(part, item_recv.at[m, q])

                @pl.when(outs[m][0])
                def _():
                    send(part, item_send.at[m, 0], item_recv.at[m, q], plane[0]).start()
                    send(part, item_send.at[m, 1], item_recv.at[m, q], plane[1]).start()

                for d in (2, 3):
                    @pl.when(outs[m][d])
                    def _():
                        send(part, item_send.at[m, d], item_recv.at[m, q], plane[d]).start()

    def near(w):
        arrived(chunk(w, z_down), z_recv.at[0, w])
        arrived(chunk(w, z_up), z_recv.at[1, w])

        @pl.when(c == 0)
        def _():
            send(chunk(w, z_down), own_send.at[2], far_recv.at[w], up).start()

        @pl.when(c == 1)
        def _():
            send(chunk(w, z_up), own_send.at[2], far_recv.at[w], down).start()

        pl.when(w + W_OPEN < NW)(lambda: send_along(w + W_OPEN))
        send(chunk(w, z_down), sib_send.at[1], sib_recv.at[w], sib).start()
        send(chunk(w, z_up), sib_send.at[1], sib_recv.at[w], sib).start()

    def exchange(t):
        third = t % 3

        @pl.when((third == W_STEP % 3) & (t >= W_STEP) & (t < W_STEP + 3 * NW))
        def _():
            near((t - W_STEP) // 3)

        @pl.when(third == W_FAR % 3)
        def _():
            @pl.when((t >= W_FAR) & (t < W_FAR + 3 * NW))
            def _():
                w = (t - W_FAR) // 3
                arrived(chunk(w, z_far), far_recv.at[w])
                send(chunk(w, z_far), sib_send.at[1], sib_recv.at[w], sib).start()

            @pl.when((t >= W_DONE) & (t < W_DONE + 3 * NW))
            def _():
                w = (t - W_DONE) // 3
                arrived(w_all.at[w, pl.ds(0, 384), :], sib_recv.at[w])

    def matrices_near():
        first, second = xh_all.at[slot(z_down), :], xh_all.at[slot(z_up), :]
        arrived(first, xz_recv.at[0])
        arrived(second, xz_recv.at[1])

        @pl.when(c == 0)
        def _():
            send(first, x_send.at[2], xf_recv, up).start()

        @pl.when(c == 1)
        def _():
            send(second, x_send.at[2], xf_recv, down).start()

        send(first, sib_send.at[2], xs_recv, sib).start()
        send(second, sib_send.at[2], xs_recv, sib).start()

    def matrices_far():
        far = xh_all.at[slot(z_far), :]
        arrived(far, xf_recv)
        send(far, sib_send.at[2], xs_recv, sib).start()

    def matrices_all():
        arrived(xh_all.at[pl.ds(0, 512), :], xs_recv)
        prepare()

    def opening(t, carry):
        pl.when(t < W_OPEN)(lambda: send_along(t))

        @pl.when(t < NW)
        def _():
            send(chunk(t, j), sib_send.at[0], own_recv.at[t], sib).start()

        @pl.when((t >= 2) & (t < 2 + NW))
        def _():
            arrived(chunk(t - 2, j_sib), own_recv.at[t - 2])

        tree(t)
        return carry

    def small_step(t, carry):
        tree(t)
        exchange(t)
        pl.when(t == X_STEP)(matrices_near)
        pl.when(t == X_FAR)(matrices_far)

        @pl.when(t >= Q_STEP)
        def _():
            pl.when(t == Q_STEP)(matrices_all)
            pl.when(t == Q_STEP + 1)(half_product)
            pl.when(t == Q_STEP + 2)(diag_product)
            pl.when(t == Q_STEP + 3)(inner_product)

            @pl.when((t >= Q_STEP + 4) & (t < Q_STEP + 8))
            def _():
                weights(t - Q_STEP - 4, True)

            pl.when(t == Q_STEP + 8)(lambda: weights(0, False))

        return carry

    def left_step(t, carry):
        tree(t)
        exchange(t)
        left_task((t - Q_STEP - 9) // 5, (t - Q_STEP - 9) % 5)
        return carry

    def trail_steps(block, carry):
        for i in range(6):
            tree(U_READY + 6 * block + i)
            if i < 4:
                trail_task(block, i)
        return carry

    lax.fori_loop(0, 10, opening, 0)
    lax.fori_loop(10, Q_STEP + 9, small_step, 0)
    lax.fori_loop(Q_STEP + 9, U_READY, left_step, 0)
    pltpu.make_async_copy(t_hbm, trail, load_sem).wait()
    lax.fori_loop(0, 7, trail_steps, 0)
    for i in range(4):
        trail_task(7, i)

    own = w_all.at[:, slot(j), :]
    done = lambda ref, sem: send(ref, sem, own_recv.at[0], sib).wait_send()
    for i in range(3):
        done(own, own_send.at[i])
        done(own_x, x_send.at[i])
    done(own, sib_send.at[0])
    done(w_all.at[:, pl.ds(0, 384), :], sib_send.at[1])
    done(xh_all.at[pl.ds(0, 512), :], sib_send.at[2])
    for m in range(2):
        for d in range(4):
            @pl.when(outs[m][d])
            def _():
                done(items.at[m], item_send.at[m, d])


def on_device(s_panel, l_inv, h_diag, h_panel, h_trail):
    vmem = pl.BlockSpec(memory_space=pltpu.VMEM)
    hbm = pl.BlockSpec(memory_space=pltpu.HBM)
    dma = pltpu.SemaphoreType.DMA
    mats = [pltpu.VMEM((NB, NB), BF16)] * 8
    low, reduced, trailing = pl.pallas_call(
        kernel,
        out_shape=(
            pltpu.VMEM(s_panel.shape[::-1], F32),
            pltpu.VMEM(h_panel.shape[::-1], F32),
            pltpu.VMEM(h_trail.shape, F32),
        ),
        in_specs=[hbm] * 5,
        out_specs=(vmem, vmem, vmem),
        scratch_shapes=[
            pltpu.VMEM((NW, 1024, 128), F32), pltpu.VMEM((1024, NB), F32),
            pltpu.VMEM((2, NW, 1024, 128), F32),
            pltpu.VMEM((ROWS, 1024), BF16), pltpu.VMEM((ROWS, 1024), BF16),
            pltpu.VMEM((1024, 1152), BF16), pltpu.VMEM((1024, 1152), BF16),
            *mats,
            pltpu.VMEM((NB, NB), F32), pltpu.VMEM((NB, 1152), BF16), pltpu.VMEM((NB, 1152), BF16),
            *[pltpu.VMEM((256, 1024), BF16)] * 2, *[pltpu.VMEM((1024, 256), BF16)] * 2,
            dma((NW,)), dma((2, NW)), dma((NW,)), dma((NW,)), dma((2, UNITS)),
            dma((2,)), dma, dma, dma((3,)), dma((3,)), dma((3,)), dma((2, 4)),
            dma((NW + 1, 2)), dma,
        ],
        compiler_params=pltpu.CompilerParams(
            collective_id=0, has_side_effects=True, vmem_limit_bytes=55 * 2**20),
        cost_estimate=pl.CostEstimate(flops=22 * 10**9, bytes_accessed=20 * 2**20, transcendentals=0),
    )(s_panel.T, l_inv.T, h_diag.T, h_panel.T, h_trail)
    return low.T, reduced.T, trailing


def solution(mesh):
    in_specs = (P("row", "col"), P(None, "col"), P(None, "col"), P("row", "col"), P("row", "col"))
    out_specs = (P("row", "col"), P("row", "col"), P("row", "col"))
    return jax.shard_map(
        on_device, mesh=mesh, in_specs=in_specs, out_specs=out_specs, check_vma=False
    )
```

time: 123 us -> 98.8 us (0.80); the launches traced: 121 us -> 98.1 us
  local copies, waits for them, and re-layouts: 19.2 us -> 4.8 us
  Pallas kernels: 101 us -> 92.7 us
    unnamed x5 -> x3, local copies, waits for them, and re-layouts: 15.3 us -> 4.8 us
    pallas_call x1, Pallas kernels: 101 us -> 92.7 us  [on_device(): pl.pallas_call(kernel, out_shape=(pltpu.VMEM(s_panel.shape[::-1], F32), p...]
    pallas_call x2 -> x0, local copies, waits for them, and re-layouts: 3.86 us -> none  [on_device(): pl.pallas_call(kernel, out_shape=(jax.ShapeDtypeStruct(s_panel.shape, F32...]
where the time goes in v2:
time: 98.8 us; the launch traced here: 98.1 us
  Pallas kernels  92.7 us (94%)
  local copies, waits for them, and re-layouts  4.8 us (5%)
    pallas_call x1, Pallas kernels, on_device(): pl.pallas_call(kernel, out_shape=(pltpu.VMEM(s_panel.shape[::-1], F32), p...  92.7 us
    unnamed x3, local copies, waits for them, and re-layouts  4.8 us

profile of v2, /device:TPU:8, one launch (start us, length us, event | category | flops | bytes accessed | tf_op | source)
XLA Modules:
  0.0 98.1 jit_solution(7765490782254062747)
XLA Ops:
  0.6 92.7 %shard_map.76 = (f32[64,1024]{1,0:T(8,128)S(1)}, f32[64,1024]{1,0:T(8,128)S(1)}, f32[1024,2048]{1,0:T(8,128)S(1)}) custom-call(f32[64,1024]{1,0:T(8,128)} %bitcast.8, f32[64,512]{1,0:T(8,128)} %bitcast.10, f32[64,512]{1,0:T(8,128)} %bitcast.11, f32[64,1024]{1,0:T(8,128)} %bitcast.9, f32[1024,2048]{1,0:T(8,128)} %t_hbm.1), custom_call_target="tpu_custom_call" | custom-call | flops 22000001024 | bytes 20971520 | tf_op jit(solution)/shard_map/pallas_call | solution.py:379
  93.3 0.7 copy.11
  94.0 0.7 copy.12
  94.7 3.4 %copy.13 = f32[1024,2048]{1,0:T(8,128)} copy(f32[1024,2048]{1,0:T(8,128)S(1)} %get-tuple-element.11) | data formatting | bytes 16777216

commit v3 on v2

--- a/solution.py
+++ b/solution.py
@@ -11,17 +11,16 @@
 F32, BF16 = jnp.float32, jnp.bfloat16
 ROWS, NB, SIDE = 1024, 512, 64
 NW = ROWS // 128
-UNITS = 64
-HOP = 5
+UNITS = 32
+HOP = 6
 LEAD = 4
-GAP = 3
-LAST = UNITS + LEAD + GAP + 4 * HOP
+GAP = 4
 W_STEP = 12
 W_FAR, W_DONE = W_STEP + 5, W_STEP + 8
 W_OPEN = 2
 X_STEP, X_FAR = W_STEP - 1, W_STEP + 4
 Q_STEP = W_DONE
-U_READY = LAST - 42
+U_READY = LEAD + GAP + 4 * HOP + 22
 
 
 def split(value):
@@ -101,16 +100,16 @@
             at(1, 0) | at(3, 0), 1, jnp.where(at(1, 1) | at(3, 3), 2, jnp.where(third, 3, 4)))))
 
     def unit(q):
-        late = q >= 16
-        block = jnp.where(late, (q + 32) // 6 - 8, q // 2)
-        which = (q + 32) % 6 // 2
+        late = q >= 8
+        block = jnp.where(late, (q + 1) // 3 - 3, q)
+        which = (q + 1) % 3
         level = jnp.where(late, jnp.where(which == 0, z + 3, jnp.where(which == 1, z + 1, z + 2)), z) % 4
-        return block, slot(level * 2 + q % 2)
+        return block, pl.ds(pl.multiple_of(level * 256, 256), 256)
 
     def unit_at(t):
         early = t < LEAD + 16
         late = t >= LEAD + 16 + GAP
-        return jnp.where(late, t - LEAD - GAP, t - LEAD), (t >= LEAD) & (early | (late & (t < LEAD + GAP + UNITS)))
+        return (t - LEAD - jnp.where(late, GAP, 0)) // 2, (t >= LEAD) & (early | (late & (t < LEAD + GAP + 2 * UNITS)))
 
     own_x = xh_all.at[slot(j), :]
     send(own_x, sib_send.at[2], xs_recv, sib).start()
@@ -174,13 +173,13 @@
                 q_low[k * 128 + shift:k * 128 + shift + SIDE, at_n] = low[k * SIDE:(k + 1) * SIDE]
 
     def left_task(g, n):
-        rows = pl.ds(pl.multiple_of(g * 256, 256), 256)
+        rows = pl.ds(pl.multiple_of(g * 512, 512), 512)
 
         @pl.when(n == 0)
         def _():
-            for h in range(2):
+            for h in range(4):
                 a_high[h * 128:h * 128 + 128, :], a_low[h * 128:h * 128 + 128, :] = split(
-                    jnp.transpose(w_all[2 * g + h]))
+                    jnp.transpose(w_all[4 * g + h]))
 
         @pl.when(n < 4)
         def _():
@@ -201,7 +200,7 @@
                 cols = pl.ds(m * 128, 128)
                 b_high[:, cols], b_low[:, cols] = split(items[m, block])
 
-        rows = pl.ds(i * 256, 256)
+        rows = pl.ds(i * 1024, 1024)
         value = dot3(left_high[rows, :], left_low[rows, :], b_high[...], b_low[...], 0)
         for m in range(2):
             cols = pl.ds(pl.multiple_of(m * ROWS + block * 128, 128), 128)
@@ -212,32 +211,34 @@
         send(chunk(w, j), own_send.at[1], z_recv.at[1, w], down).start()
 
     def tree(t):
-        for m in range(2):
-            q_copy, ready = unit_at(t + 2)
-
-            @pl.when((depth[m] == 0) & ready)
+        m = t % 2
+        mine = lambda pair: jnp.where(m == 0, pair[0].astype(jnp.int32), pair[1].astype(jnp.int32))
+        level = mine(depth)
+        q_copy, ready = unit_at(t + 2 - m)
+
+        @pl.when((level == 0) & ready)
+        def _():
+            at = unit(q_copy)
+            pltpu.make_async_copy(
+                w_all.at[at[0], at[1], :], items.at[m, at[0], at[1], :], item_recv.at[m, q_copy]).start()
+
+        q, here = unit_at(t - m - HOP * level)
+
+        @pl.when(here)
+        def _():
+            at = unit(q)
+            part = items.at[m, at[0], at[1], :]
+            arrived(part, item_recv.at[m, q])
+
+            @pl.when(mine([outs[0][0], outs[1][0]]) == 1)
             def _():
-                at = unit(q_copy)
-                pltpu.make_async_copy(
-                    w_all.at[at[0], at[1], :], items.at[m, at[0], at[1], :], item_recv.at[m, q_copy]).start()
-
-            q, here = unit_at(t - HOP * depth[m])
-
-            @pl.when(here)
-            def _():
-                at = unit(q)
-                part = items.at[m, at[0], at[1], :]
-                arrived(part, item_recv.at[m, q])
-
-                @pl.when(outs[m][0])
+                send(part, item_send.at[m, 0], item_recv.at[m, q], plane[0]).start()
+                send(part, item_send.at[m, 1], item_recv.at[m, q], plane[1]).start()
+
+            for d in (2, 3):
+                @pl.when(mine([outs[0][d], outs[1][d]]) == 1)
                 def _():
-                    send(part, item_send.at[m, 0], item_recv.at[m, q], plane[0]).start()
-                    send(part, item_send.at[m, 1], item_recv.at[m, q], plane[1]).start()
-
-                for d in (2, 3):
-                    @pl.when(outs[m][d])
-                    def _():
-                        send(part, item_send.at[m, d], item_recv.at[m, q], plane[d]).start()
+                    send(part, item_send.at[m, d], item_recv.at[m, q], plane[d]).start()
 
     def near(w):
         arrived(chunk(w, z_down), z_recv.at[0, w])
@@ -338,13 +339,19 @@
     def left_step(t, carry):
         tree(t)
         exchange(t)
-        left_task((t - Q_STEP - 9) // 5, (t - Q_STEP - 9) % 5)
+
+        past = t - Q_STEP - 10
+
+        @pl.when((past >= 0) & (past % 2 == 0) & (past % 12 < 10))
+        def _():
+            left_task(past // 12, past % 12 // 2)
+
         return carry
 
     def trail_steps(block, carry):
         for i in range(6):
             tree(U_READY + 6 * block + i)
-            if i < 4:
+            if i == 0:
                 trail_task(block, i)
         return carry
 
@@ -353,7 +360,7 @@
     lax.fori_loop(Q_STEP + 9, U_READY, left_step, 0)
     pltpu.make_async_copy(t_hbm, trail, load_sem).wait()
     lax.fori_loop(0, 7, trail_steps, 0)
-    for i in range(4):
+    for i in range(1):
         trail_task(7, i)
 
     own = w_all.at[:, slot(j), :]
@@ -392,7 +399,7 @@
             pltpu.VMEM((1024, 1152), BF16), pltpu.VMEM((1024, 1152), BF16),
             *mats,
             pltpu.VMEM((NB, NB), F32), pltpu.VMEM((NB, 1152), BF16), pltpu.VMEM((NB, 1152), BF16),
-            *[pltpu.VMEM((256, 1024), BF16)] * 2, *[pltpu.VMEM((1024, 256), BF16)] * 2,
+            *[pltpu.VMEM((512, 1024), BF16)] * 2, *[pltpu.VMEM((1024, 256), BF16)] * 2,
             dma((NW,)), dma((2, NW)), dma((NW,)), dma((NW,)), dma((2, UNITS)),
             dma((2,)), dma, dma, dma((3,)), dma((3,)), dma((3,)), dma((2, 4)),
             dma((NW + 1, 2)), dma,

time: 98.8 us -> 92.9 us (0.940)
  Pallas kernels: 92.7 us -> 87.4 us
    pallas_call x1, Pallas kernels: 92.7 us -> 87.4 us  [on_device(): pl.pallas_call(kernel, out_shape=(pltpu.VMEM(s_panel.shape[::-1], F32), p...]
where the time goes in v3:
time: 92.9 us; the launch traced here: 92.8 us
  Pallas kernels  87.4 us (94%)
  local copies, waits for them, and re-layouts  4.8 us (5%)
    pallas_call x1, Pallas kernels, on_device(): pl.pallas_call(kernel, out_shape=(pltpu.VMEM(s_panel.shape[::-1], F32), p...  87.4 us
    unnamed x3, local copies, waits for them, and re-layouts  4.8 us

profile of v3, /device:TPU:8, one launch (start us, length us, event | category | flops | bytes accessed | tf_op | source)
XLA Modules:
  0.0 92.8 jit_solution(6750754307736111620)
XLA Ops:
  0.6 87.4 %shard_map.76 = (f32[64,1024]{1,0:T(8,128)S(1)}, f32[64,1024]{1,0:T(8,128)S(1)}, f32[1024,2048]{1,0:T(8,128)S(1)}) custom-call(f32[64,1024]{1,0:T(8,128)} %bitcast.8, f32[64,512]{1,0:T(8,128)} %bitcast.10, f32[64,512]{1,0:T(8,128)} %bitcast.11, f32[64,1024]{1,0:T(8,128)} %bitcast.9, f32[1024,2048]{1,0:T(8,128)} %t_hbm.1), custom_call_target="tpu_custom_call" | custom-call | flops 22000001024 | bytes 20971520 | tf_op jit(solution)/shard_map/pallas_call | solution.py:386
  88.0 0.7 copy.11
  88.7 0.7 copy.12
  89.4 3.4 %copy.13 = f32[1024,2048]{1,0:T(8,128)} copy(f32[1024,2048]{1,0:T(8,128)S(1)} %get-tuple-element.11) | data formatting | bytes 16777216

commit v4 on v3

--- a/solution.py
+++ b/solution.py
@@ -21,6 +21,8 @@
 X_STEP, X_FAR = W_STEP - 1, W_STEP + 4
 Q_STEP = W_DONE
 U_READY = LEAD + GAP + 4 * HOP + 22
+LEFT_STEP = Q_STEP + 18
+TRAIL_STEP = U_READY + 7
 
 
 def split(value):
@@ -321,18 +323,20 @@
         pl.when(t == X_STEP)(matrices_near)
         pl.when(t == X_FAR)(matrices_far)
 
-        @pl.when(t >= Q_STEP)
-        def _():
-            pl.when(t == Q_STEP)(matrices_all)
-            pl.when(t == Q_STEP + 1)(half_product)
-            pl.when(t == Q_STEP + 2)(diag_product)
-            pl.when(t == Q_STEP + 3)(inner_product)
-
-            @pl.when((t >= Q_STEP + 4) & (t < Q_STEP + 8))
+        task, rest = (t - Q_STEP) // 2, (t - Q_STEP) % 2
+
+        @pl.when((t >= Q_STEP) & (rest == 0))
+        def _():
+            pl.when(task == 0)(matrices_all)
+            pl.when(task == 1)(half_product)
+            pl.when(task == 2)(diag_product)
+            pl.when(task == 3)(inner_product)
+
+            @pl.when((task >= 4) & (task < 8))
             def _():
-                weights(t - Q_STEP - 4, True)
-
-            pl.when(t == Q_STEP + 8)(lambda: weights(0, False))
+                weights(task - 4, True)
+
+            pl.when(task == 8)(lambda: weights(0, False))
 
         return carry
 
@@ -340,28 +344,44 @@
         tree(t)
         exchange(t)
 
-        past = t - Q_STEP - 10
-
-        @pl.when((past >= 0) & (past % 2 == 0) & (past % 12 < 10))
-        def _():
-            left_task(past // 12, past % 12 // 2)
+        past = t - LEFT_STEP
+        task = past // 5 * 2 + past % 5 // 2
+
+        @pl.when((past % 5 == 0) | (past % 5 == 2))
+        def _():
+            left_task(task // 5, task % 5)
 
         return carry
 
+    def last_block(k, carry):
+        at_k = pl.ds(pl.multiple_of((z + 3 + k) % 4 * 256, 256), 256)
+        for m in range(2):
+            cols = pl.ds(m * 128, 128)
+            b_high[:256, cols], b_low[:256, cols] = split(items[m, NW - 1, at_k, :])
+        value = dot3(left_high[:, at_k], left_low[:, at_k], b_high[:256, :], b_low[:256, :], 0)
+        for m in range(2):
+            cols = pl.ds((m + 1) * ROWS - 128, 128)
+            trail[:, cols] = trail[:, cols] - value[:, m * 128:m * 128 + 128]
+        return carry
+
+    def most_of_last():
+        lax.fori_loop(0, 3, last_block, 0)
+
     def trail_steps(block, carry):
-        for i in range(6):
-            tree(U_READY + 6 * block + i)
+        for i in range(5):
+            tree(TRAIL_STEP + 5 * block + i)
             if i == 0:
                 trail_task(block, i)
+            if i == 3:
+                pl.when(block == 6)(most_of_last)
         return carry
 
     lax.fori_loop(0, 10, opening, 0)
-    lax.fori_loop(10, Q_STEP + 9, small_step, 0)
-    lax.fori_loop(Q_STEP + 9, U_READY, left_step, 0)
+    lax.fori_loop(10, LEFT_STEP, small_step, 0)
+    lax.fori_loop(LEFT_STEP, TRAIL_STEP, left_step, 0)
     pltpu.make_async_copy(t_hbm, trail, load_sem).wait()
     lax.fori_loop(0, 7, trail_steps, 0)
-    for i in range(1):
-        trail_task(7, i)
+    last_block(3, None)
 
     own = w_all.at[:, slot(j), :]
     done = lambda ref, sem: send(ref, sem, own_recv.at[0], sib).wait_send()

time: 92.9 us -> 92.1 us (level)
  no operation moved by 1% of the time
where the time goes in v4:
time: 92.1 us; the launch traced here: 92 us
  Pallas kernels  86.6 us (94%)
  local copies, waits for them, and re-layouts  4.8 us (5%)
    pallas_call x1, Pallas kernels, on_device(): pl.pallas_call(kernel, out_shape=(pltpu.VMEM(s_panel.shape[::-1], F32), p...  86.6 us
    unnamed x3, local copies, waits for them, and re-layouts  4.8 us

profile of v4, /device:TPU:8, one launch (start us, length us, event | category | flops | bytes accessed | tf_op | source)
XLA Modules:
  0.0 92.0 jit_solution(12959084828462015494)
XLA Ops:
  0.6 86.6 %shard_map.76 = (f32[64,1024]{1,0:T(8,128)S(1)}, f32[64,1024]{1,0:T(8,128)S(1)}, f32[1024,2048]{1,0:T(8,128)S(1)}) custom-call(f32[64,1024]{1,0:T(8,128)} %bitcast.8, f32[64,512]{1,0:T(8,128)} %bitcast.10, f32[64,512]{1,0:T(8,128)} %bitcast.11, f32[64,1024]{1,0:T(8,128)} %bitcast.9, f32[1024,2048]{1,0:T(8,128)} %t_hbm.1), custom_call_target="tpu_custom_call" | custom-call | flops 22000001024 | bytes 20971520 | tf_op jit(solution)/shard_map/pallas_call | solution.py:406
  87.2 0.7 copy.11
  87.9 0.7 copy.12
  88.6 3.4 %copy.13 = f32[1024,2048]{1,0:T(8,128)} copy(f32[1024,2048]{1,0:T(8,128)S(1)} %get-tuple-element.11) | data formatting | bytes 16777216
